TPU v7x, 512 devices: a whole 4x4x16 slice. The times are simulated.
512 devices in a mesh: space: 64 (over y, z), dp: 8 (over x, core).
Axes of the slice: x: 4, y: 4, z: 16, core: 2. Of those that a mesh axis runs over, the one named last changes fastest.
Arguments:
- coarse_latents: bfloat16 [8, 4096, 512], P('dp', 'space'), may hold values from -6 to 6
- active_blocks: int32 [8, 128], P('dp'), may hold values from 0 to 4095, as said below
- face_links: int32 [8, 128, 6], P('dp', 'space'), may hold values from -1 to 127, as said below
- cotangent: bfloat16 [8, 128, 8, 8, 256], P('dp', 'space'), may hold values from -6 to 6
- up_weight: bfloat16 [64, 2048], replicated, may hold values from -0.75 to 0.75
- conv_one: bfloat16 [27, 32, 32], replicated, may hold values from -0.21875 to 0.21875
- conv_two: bfloat16 [27, 32, 32], replicated, may hold values from -0.21875 to 0.21875
Outputs:
- fine: bfloat16 [8, 128, 8, 8, 256], P('dp', 'space')
- grad_one: float32 [27, 32, 32], replicated
- grad_two: float32 [27, 32, 32], replicated
Inputs may be any that keep to these rules, and one draw needn't show every extreme that they name: `active_blocks`: call the bricks at positions i * 2 to (i + 1) * 2 - 1 group i and the block rows i * 64 to (i + 1) * 64 - 1 range i. At most 2 bricks of one group take their blocks from one range, and in every scene every group has exactly 2 from some range. `face_links`: links are mutual: if brick h is the neighbour of g across face f, g is the neighbour of h across the opposite face. A neighbour of brick g lies at a position whose quotient by 2 differs from that of g by at most one; across a -x, -y or -z face that quotient is never larger than that of g, across a +x, +y or +z face never smaller.
All inputs are finite; a program needn't handle non-finite values.
Results may differ from a plain program's by a relative error of at most 0.0057.
Values may be sent and summed in bfloat16 or wider, within the bound.
A program may use at most 128 MiB of HBM per device.

v0:
```python
import math
import jax
import jax.numpy as jnp
from jax import lax
from jax.sharding import PartitionSpec as P


def passed_along(value, axis, steps):
    count = lax.axis_size(axis)
    first, last = (max(0, -steps), min(count, count - steps))
    return lax.ppermute(value, axis, [(source, source + steps) for source in range(first, last)])


def depth_select(extent):
    inputs_z = jnp.arange(extent + 2)[None, :, None]
    outputs_z = jnp.arange(extent)[None, None, :]
    offsets_z = jnp.arange(3)[:, None, None]
    return (inputs_z == outputs_z + offsets_z).astype(jnp.float32)


def band_matrix(weights, extent):
    channels = weights.shape[1]
    cube = weights.astype(jnp.float32).reshape(3, 3, 3, channels, channels)
    banded = jnp.einsum(
        "dpq,abdio->abpiqo", depth_select(extent), cube, precision=lax.Precision.HIGHEST
    )
    return banded.reshape(3, 3, (extent + 2) * channels, extent * channels).astype(jnp.bfloat16)


def apply_band(padded, banded, extent):
    total = None
    for shift_x in range(3):
        for shift_y in range(3):
            window = padded[:, shift_x : shift_x + extent, shift_y : shift_y + extent, :]
            term = jnp.einsum(
                "nxyp,pq->nxyq",
                window,
                banded[shift_x, shift_y],
                preferred_element_type=jnp.float32,
            )
            total = term if total is None else total + term
    return total


def band_gradient(padded, gradient, extent, channels):
    select = depth_select(extent)
    pieces = []
    for shift_x in range(3):
        for shift_y in range(3):
            window = padded[:, shift_x : shift_x + extent, shift_y : shift_y + extent, :]
            outer = jnp.einsum(
                "nxyp,nxyq->pq", window, gradient, preferred_element_type=jnp.float32
            )
            outer = outer.reshape(extent + 2, channels, extent, channels)
            pieces.append(
                jnp.einsum("dpq,piqo->dio", select, outer, precision=lax.Precision.HIGHEST)
            )
    return jnp.stack(pieces).reshape(27, channels, channels)


def lift_bricks(latent_rows, up_weight, extent, channels):
    bricks_here = latent_rows.shape[0]
    blocks = latent_rows.reshape(bricks_here, 8, -1)
    cells = jnp.einsum("nci,io->nco", blocks, up_weight, preferred_element_type=jnp.float32)
    half = extent // 2
    shaped = cells.reshape(bricks_here, 2, 2, 2, half, half, half, channels)
    shaped = shaped.transpose(0, 1, 4, 2, 5, 3, 6, 7)
    return shaped.reshape(bricks_here, extent, extent, extent * channels).astype(jnp.bfloat16)


def face_planes(volume, channels):
    bricks_here, extent = (volume.shape[0], volume.shape[1])
    planes = [
        volume[:, 0],
        volume[:, extent - 1],
        volume[:, :, 0],
        volume[:, :, extent - 1],
        volume[:, :, :, 0:channels],
        volume[:, :, :, (extent - 1) * channels :],
    ]
    return jnp.stack([one_plane.reshape(bricks_here, -1) for one_plane in planes], axis=1)


def share_faces(stacked):
    from_left = passed_along(stacked, "space", 1)
    from_right = passed_along(stacked, "space", -1)
    return jnp.stack([from_left, stacked, from_right], axis=1)


def fill_padding(volume, face_pool, face_links, position, channels):
    bricks_here, extent = (volume.shape[0], volume.shape[1])
    neighbour = jnp.maximum(face_links, 0)
    source = jnp.clip(neighbour // bricks_here - position + 1, 0, 2)
    face_index = jnp.arange(6, dtype=jnp.int32)[None, :]
    row_index = (source * bricks_here + neighbour % bricks_here) * 6 + (face_index ^ 1)
    flattened = face_pool.reshape(3 * bricks_here * 6, -1)
    picked = jnp.take(flattened, row_index.reshape(-1), axis=0).reshape(bricks_here, 6, -1)
    picked = jnp.where((face_links >= 0)[:, :, None], picked, jnp.zeros((), picked.dtype))
    padded = jnp.pad(volume, ((0, 0), (1, 1), (1, 1), (channels, channels)))
    inside_range = slice(1, extent + 1)
    middle_range = slice(channels, (extent + 1) * channels)
    flat_face = (bricks_here, extent, extent * channels)
    depth_face = (bricks_here, extent, extent, channels)
    padded = padded.at[:, 0, inside_range, middle_range].set(picked[:, 0].reshape(flat_face))
    padded = padded.at[:, extent + 1, inside_range, middle_range].set(
        picked[:, 1].reshape(flat_face)
    )
    padded = padded.at[:, inside_range, 0, middle_range].set(picked[:, 2].reshape(flat_face))
    padded = padded.at[:, inside_range, extent + 1, middle_range].set(
        picked[:, 3].reshape(flat_face)
    )
    padded = padded.at[:, inside_range, inside_range, 0:channels].set(
        picked[:, 4].reshape(depth_face)
    )
    padded = padded.at[:, inside_range, inside_range, (extent + 1) * channels :].set(
        picked[:, 5].reshape(depth_face)
    )
    return padded


def body(coarse_latents, active_blocks, face_links, cotangent, up_weight, conv_one, conv_two):
    position = lax.axis_index("space")
    devices = lax.axis_size("space")
    bricks_here = face_links.shape[1]
    extent = cotangent.shape[2]
    channels = conv_one.shape[1]
    blocks_here = coarse_latents.shape[1]
    local_rows = coarse_latents[0]
    listed = active_blocks[0]
    mine = lax.dynamic_slice_in_dim(listed, position * bricks_here, bricks_here)
    owners = mine // blocks_here
    wanted = listed.reshape(devices, bricks_here)
    held = wanted // blocks_here == position
    local_index = jnp.clip(wanted - position * blocks_here, 0, blocks_here - 1)
    packed = jnp.where(
        held[:, :, None], jnp.take(local_rows, local_index, axis=0), jnp.zeros((), local_rows.dtype)
    )
    received = lax.all_to_all(packed, "space", split_axis=0, concat_axis=0, tiled=True)
    latent_rows = received[owners, jnp.arange(bricks_here)]
    lifted = lift_bricks(latent_rows, up_weight, extent, channels)
    links = face_links[0]
    upstream = cotangent[0]
    lifted_pool = share_faces(face_planes(lifted, channels)[None])[0]
    lifted_pad = fill_padding(lifted, lifted_pool, links, position, channels)
    band_one = band_matrix(conv_one, extent)
    band_two = band_matrix(conv_two, extent)
    band_back = band_matrix(jnp.flip(conv_two, axis=0).transpose(0, 2, 1), extent)
    pre = apply_band(lifted_pad, band_one, extent)
    hidden = jax.nn.silu(pre).astype(jnp.bfloat16)
    hidden_pool = share_faces(face_planes(hidden, channels)[None])[0]
    hidden_pad = fill_padding(hidden, hidden_pool, links, position, channels)
    fine = (lifted.astype(jnp.float32) + apply_band(hidden_pad, band_two, extent)).astype(
        jnp.bfloat16
    )
    scale = 1.0 / math.sqrt(lax.axis_size("dp") * devices * bricks_here * extent**3)
    second_local = band_gradient(hidden_pad, upstream, extent, channels) * scale
    upstream_pool = share_faces(face_planes(upstream, channels)[None])[0]
    upstream_pad = fill_padding(upstream, upstream_pool, links, position, channels)
    back = apply_band(upstream_pad, band_back, extent)
    sigmoid = jax.nn.sigmoid(pre)
    grad_pre = (back * sigmoid * (1.0 + pre * (1.0 - sigmoid))).astype(jnp.bfloat16)
    first_local = band_gradient(lifted_pad, grad_pre, extent, channels) * scale
    grad_one, grad_two = lax.psum((first_local, second_local), ("space", "dp"))
    return (fine[None], grad_one, grad_two)


def solution(mesh):
    return jax.shard_map(
        body,
        mesh=mesh,
        in_specs=(
            P("dp", "space", None),
            P("dp", None),
            P("dp", "space", None),
            P("dp", "space", None, None, None),
            P(),
            P(),
            P(),
        ),
        out_specs=(P("dp", "space", None, None, None), P(), P()),
        check_vma=False,
    )
```

profile of v0, /device:TPU:1, one launch (start us, length us, event | category | flops | bytes accessed | tf_op | source)
XLA Modules:
  0.0 758.2 jit_solution(1332796535409045901)
XLA Ops:
  13.7 5.0 collective-permute-start.4
  25.9 19.5 %all-to-all-start = ((bf16[64,2,512]{2,1,0:T(2,128)(2,1)}), bf16[64,2,512]{2,1,0:T(2,128)(2,1)S(1)}, u32[]{:S(2)}, u32[]{:S(2)}) async-start(bf16[64,2,512]{2,1,0:T(2,128)(2,1)} %broadcast_select_fusion.1), calls=%async_computation | async-start | bytes 262144 | tf_op jit(solution)/shard_map/all_to_all | solution.py:138
  45.5 5.6 convert_bitcast_fusion.2
  51.7 5.7 convert_bitcast_fusion
  57.4 2.0 all-to-all-done
  65.3 3.2 collective-permute-start
  70.2 5.6 convert_bitcast_fusion.1
  75.8 10.3 %copy.127 = bf16[3,3,10,32,8,32]{5,4,3,2,1,0:T(8,128)(2,1)} copy(bf16[3,3,10,32,8,32]{5,2,3,1,0,4:T(8,128)(2,1)} %convert_bitcast_fusion.2) | data formatting | bytes 2949120 | tf_op jit(solution)/shard_map/convert_element_type | solution.py:27
  86.2 7.2 convert_element_type.66
  93.7 10.3 %copy.141 = bf16[3,3,10,32,8,32]{5,4,3,2,1,0:T(8,128)(2,1)} copy(bf16[3,3,10,32,8,32]{5,2,3,1,0,4:T(8,128)(2,1)} %convert_bitcast_fusion) | data formatting | bytes 2949120 | tf_op jit(solution)/shard_map/convert_element_type | solution.py:27
  103.9 8.3 %convert_element_type.74 = bf16[3,3,320,256]{3,2,1,0:T(8,128)(2,1)} reshape(bf16[3,3,10,32,8,32]{5,4,3,2,1,0:T(8,128)(2,1)} %copy.141) | data formatting | bytes 2949120 | tf_op jit(solution)/shard_map/convert_element_type | solution.py:27
  112.2 10.4 %copy.134 = bf16[3,3,10,32,8,32]{5,4,3,2,1,0:T(8,128)(2,1)} copy(bf16[3,3,10,32,8,32]{5,2,3,1,0,4:T(8,128)(2,1)} %convert_bitcast_fusion.1) | data formatting | bytes 2949120 | tf_op jit(solution)/shard_map/convert_element_type | solution.py:27
  122.6 7.2 convert_element_type.70
  134.0 2.2 gather_fusion.2
  142.1 3.0 scatter.60
  145.1 2.9 scatter.61
  148.0 4.0 scatter.64
  152.0 4.0 scatter.65
  156.0 2.9 scatter.66
  158.9 5.7 scatter.69
  170.3 4.0 collective-permute-start.2
  182.9 2.7 scatter.84
  185.6 2.7 scatter.85
  189.0 5.0 scatter.89
  215.4 2.7 scatter.74
  218.1 2.7 scatter.75
  221.5 5.4 scatter.79
  231.5 2.2 fusion.72
  235.2 2.2 fusion.75
  239.0 2.2 fusion.78
  274.7 2.2 fusion.45
  283.1 464.4 %all-reduce.6.cloned.1.call-done = (f32[27,32,32]{2,1,0:T(8,128)}, f32[27,32,32]{2,1,0:T(8,128)}) async-done(((f32[27,32,32]{2,1,0:T(8,128)}, f32[27,32,32]{2,1,0:T(8,128)}), (f32[27,32,32]{2,1,0:T(8,128)}, f32[27,32,32]{2,1,0:T(8,128)})) %all-reduce.6.cloned.1.call-update) | async-done | bytes 221200 | tf_op jit(solution)/shard_map/psum | solution.py:163
  (269 shorter events, 119.6 us)
Async XLA Ops:
  7.2 16.7 %copy-start = (bf16[1,64,512]{2,1,0:T(8,128)(2,1)S(1)}, bf16[1,64,512]{2,1,0:T(8,128)(2,1)}, u32[]{:S(2)}) copy-start(bf16[1,64,512]{2,1,0:T(8,128)(2,1)} %param.45) | copy-start | bytes 196612
  7.2 38.3 %copy-start.8 = (bf16[27,32,32]{2,1,0:T(8,128)(2,1)S(1)}, bf16[27,32,32]{2,1,0:T(8,128)(2,1)}, u32[]{:S(2)}) copy-start(bf16[27,32,32]{2,1,0:T(8,128)(2,1)} %param.50) | copy-start | bytes 165892
  13.7 162.2 %collective-permute-start.4 = (bf16[1,2,6,2048]{3,1,2,0:T(2,128)(2,1)}, bf16[1,2,6,2048]{3,1,2,0:T(2,128)(2,1)}, u32[]{:S(2)}, u32[]{:S(2)}) collective-permute-start(bf16[1,2,6,2048]{3,1,2,0:T(2,128)(2,1)} %bitcast.92), channel_id=1, source_target_pairs={{0,8},{8,16},{16,24},{24,32},{32,40},{40,48},{48,56},{56,64},{64,7... | collective-permute-start | bytes 147464 | tf_op jit(solution)/shard_map/ppermute | solution.py:11
  18.7 157.2 %collective-permute-start.5 = (bf16[1,2,6,2048]{3,1,2,0:T(2,128)(2,1)}, bf16[1,2,6,2048]{3,1,2,0:T(2,128)(2,1)}, u32[]{:S(2)}, u32[]{:S(2)}) collective-permute-start(bf16[1,2,6,2048]{3,1,2,0:T(2,128)(2,1)} %bitcast.92), channel_id=1, source_target_pairs={{8,0},{16,8},{24,16},{32,24},{40,32},{48,40},{56,48},{64,56},{72,6... | collective-permute-start | bytes 147464 | tf_op jit(solution)/shard_map/ppermute | solution.py:11
  21.3 116.5 %copy-start.16 = (pred[2,6]{1,0:T(4,128)(4,1)}, pred[2,6]{1,0:T(4,128)(4,1)S(1)}, u32[]{:S(2)}) copy-start(pred[2,6]{1,0:T(4,128)(4,1)S(1)} %get-tuple-element.285) | copy-start | bytes 40
  23.8 112.4 %copy-start.14 = (pred[12]{0:T(512)(128)(4,1)}, pred[12]{0:T(512)(128)(4,1)S(1)}, u32[]{:S(2)}) copy-start(pred[12]{0:T(512)(128)(4,1)S(1)} %get-tuple-element.242) | copy-start | bytes 40
  25.9 33.5 %all-to-all-start = ((bf16[64,2,512]{2,1,0:T(2,128)(2,1)}), bf16[64,2,512]{2,1,0:T(2,128)(2,1)S(1)}, u32[]{:S(2)}, u32[]{:S(2)}) async-start(bf16[64,2,512]{2,1,0:T(2,128)(2,1)} %broadcast_select_fusion.1), calls=%async_computation | async-start | bytes 262144 | tf_op jit(solution)/shard_map/all_to_all | solution.py:138
  45.4 702.1 %all-reduce.6.cloned.1.call-start = ((), (), s32[]{:S(2)}) async-start(), calls=%async_computation.1 | async-start | bytes 1769472 | tf_op jit(solution)/shard_map/psum | solution.py:163
  45.5 5.6 copy-start.18
  45.5 5.7 copy-start.9
  45.5 6.0 copy-start.6
  61.2 68.5 %copy-start.4 = (bf16[2,8,8,256]{3,2,1,0:T(8,128)(2,1)}, bf16[2,8,8,256]{3,2,1,0:T(8,128)(2,1)S(1)}, u32[]{:S(2)}) copy-start(bf16[2,8,8,256]{3,2,1,0:T(8,128)(2,1)S(1)} %convert_element_type.62) | copy-start | bytes 196612
  65.3 65.3 %collective-permute-start = (bf16[1,2,6,2048]{3,1,2,0:T(2,128)(2,1)}, bf16[1,2,6,2048]{3,1,2,0:T(2,128)(2,1)}, u32[]{:S(2)}, u32[]{:S(2)}) collective-permute-start(bf16[1,2,6,2048]{3,1,2,0:T(2,128)(2,1)} %bitcast.10), channel_id=1, source_target_pairs={{0,8},{8,16},{16,24},{24,32},{32,40},{40,48},{48,56},{56,64},{64,7... | collective-permute-start | bytes 147464 | tf_op jit(solution)/shard_map/ppermute | solution.py:11
  68.5 62.1 %collective-permute-start.1 = (bf16[1,2,6,2048]{3,1,2,0:T(2,128)(2,1)}, bf16[1,2,6,2048]{3,1,2,0:T(2,128)(2,1)}, u32[]{:S(2)}, u32[]{:S(2)}) collective-permute-start(bf16[1,2,6,2048]{3,1,2,0:T(2,128)(2,1)} %bitcast.10), channel_id=1, source_target_pairs={{8,0},{16,8},{24,16},{32,24},{40,32},{48,40},{56,48},{64,56},{72,6... | collective-permute-start | bytes 147464 | tf_op jit(solution)/shard_map/ppermute | solution.py:11
  86.2 7.2 copy-start.7
  164.6 3.4 copy-start.2
  170.3 7.5 collective-permute-start.2
  174.3 4.8 collective-permute-start.3
  177.0 3.1 copy-start.15
  177.1 3.2 copy-start.17
  196.2 6.7 copy-start.19
  199.6 4.5 copy-start.3
  250.8 1.6 copy-start.10
  250.9 1.6 copy-start.11
  250.9 1.6 copy-start.12
  278.2 1.6 copy-start.13
  281.5 0.8 copy-start.5
  282.2 468.9 %copy-start.1 = (bf16[1,64,512]{2,1,0:T(8,128)(2,1)S(1)}, bf16[1,64,512]{2,1,0:T(8,128)(2,1)}, u32[]{:S(2)}) copy-start(bf16[1,64,512]{2,1,0:T(8,128)(2,1)} %param.45) | copy-start | bytes 196612
Sparse Core Ops, SparseCore 0:
  282.4 465.0 all-reduce.5
where the time goes:
time: 766 us; the launch traced here: 758 us
  waiting for transfers between devices  468 us (61%)
  local copies, waits for them, and re-layouts  151 us (20%)
  matrix products  77.9 us (10%)
  starting transfers between devices  36.3 us (5%)
  between operations  15.5 us (2%)
  other arithmetic  9.85 us (1%)
    psum x1, waiting for transfers between devices, body(): grad_one, grad_two = lax.psum((first_local, second_local), ('space', 'dp'))  464 us
    convert_element_type x6, local copies, waits for them, and re-layouts, band_matrix(): banded.reshape(3, 3, (extent + 2) * channels, extent * channels)  53.6 us
    dot_general x18, matrix products, band_gradient(): jnp.einsum('dpq,piqo->dio', select, outer, precision=lax.Precision.HIGHEST)  30.7 us
    all_to_all x1, starting transfers between devices, body(): lax.all_to_all(packed, 'space', split_axis=0, concat_axis=0, tiled=True)  19.5 us
    dot_general x27, matrix products, apply_band(): jnp.einsum('nxyp,pq->nxyq', window, banded[shift_x, shift_y], preferred_e...  17.4 us
    dot_general x3, matrix products, band_matrix(): jnp.einsum('dpq,abdio->abpiqo', depth_select(extent), cube, precision=lax...  16.8 us
    ppermute x6, starting transfers between devices, passed_along(): lax.ppermute(value, axis, [(source, source + steps) for source in range(f...  16.7 us
    scatter x3, local copies, waits for them, and re-layouts, fill_padding(): padded.at[:, inside_range, inside_range, (extent + 1) * channels:]  16.1 us
  transfers between devices with their start and end apart: 8, of which 3 were waited for; matrix products, arithmetic and copies ran while one was open for 17% of the time, Pallas kernels for 0%

commit v1 on v0

--- a/solution.py
+++ b/solution.py
@@ -160,7 +160,7 @@
     sigmoid = jax.nn.sigmoid(pre)
     grad_pre = (back * sigmoid * (1.0 + pre * (1.0 - sigmoid))).astype(jnp.bfloat16)
     first_local = band_gradient(lifted_pad, grad_pre, extent, channels) * scale
-    grad_one, grad_two = lax.psum((first_local, second_local), ("space", "dp"))
+    grad_one, grad_two = lax.psum(lax.psum((first_local, second_local), "space"), "dp")
     return (fine[None], grad_one, grad_two)
 
 

time: 766 us -> 649 us (0.85)
  waiting for transfers between devices: 468 us -> 350 us
    psum x1 -> x2, waiting for transfers between devices: 464 us -> 347 us  [the longest x1 264 us: body(): lax.psum((first_local, second_local), 'space')]
  transfers between devices with their start and end apart: 8 -> 9, of which waited for: 3 -> 4; matrix products, arithmetic and copies ran while one was open for 17% -> 20% of each run, Pallas kernels for 0% -> 0%
where the time goes in v1:
time: 649 us; the launch traced here: 640 us
  waiting for transfers between devices  350 us (54%)
  local copies, waits for them, and re-layouts  151 us (23%)
  matrix products  77.9 us (12%)
  starting transfers between devices  36.3 us (6%)
  between operations  15.5 us (2%)
  other arithmetic  9.85 us (2%)
    psum x1, waiting for transfers between devices, body(): lax.psum((first_local, second_local), 'space')  264 us
    psum x1, waiting for transfers between devices, body(): lax.psum(lax.psum((first_local, second_local), 'space'), 'dp')  82.5 us
    convert_element_type x6, local copies, waits for them, and re-layouts, band_matrix(): banded.reshape(3, 3, (extent + 2) * channels, extent * channels)  53.6 us
    dot_general x18, matrix products, band_gradient(): jnp.einsum('dpq,piqo->dio', select, outer, precision=lax.Precision.HIGHEST)  30.7 us
    all_to_all x1, starting transfers between devices, body(): lax.all_to_all(packed, 'space', split_axis=0, concat_axis=0, tiled=True)  19.5 us
    dot_general x27, matrix products, apply_band(): jnp.einsum('nxyp,pq->nxyq', window, banded[shift_x, shift_y], preferred_e...  17.4 us
    dot_general x3, matrix products, band_matrix(): jnp.einsum('dpq,abdio->abpiqo', depth_select(extent), cube, precision=lax...  16.8 us
    ppermute x6, starting transfers between devices, passed_along(): lax.ppermute(value, axis, [(source, source + steps) for source in range(f...  16.7 us
  transfers between devices with their start and end apart: 9, of which 4 were waited for; matrix products, arithmetic and copies ran while one was open for 20% of the time, Pallas kernels for 0%

profile of v1, /device:TPU:1, one launch (start us, length us, event | category | flops | bytes accessed | tf_op | source)
XLA Modules:
  0.0 640.4 jit_solution(1209141624925303716)
XLA Ops:
  13.7 5.0 collective-permute-start.4
  25.9 19.5 %all-to-all-start = ((bf16[64,2,512]{2,1,0:T(2,128)(2,1)}), bf16[64,2,512]{2,1,0:T(2,128)(2,1)S(1)}, u32[]{:S(2)}, u32[]{:S(2)}) async-start(bf16[64,2,512]{2,1,0:T(2,128)(2,1)} %broadcast_select_fusion.1), calls=%async_computation | async-start | bytes 262144 | tf_op jit(solution)/shard_map/all_to_all | solution.py:138
  45.5 5.6 convert_bitcast_fusion.2
  51.7 5.7 convert_bitcast_fusion
  65.3 3.2 collective-permute-start
  70.2 5.6 convert_bitcast_fusion.1
  75.8 10.3 %copy.127 = bf16[3,3,10,32,8,32]{5,4,3,2,1,0:T(8,128)(2,1)} copy(bf16[3,3,10,32,8,32]{5,2,3,1,0,4:T(8,128)(2,1)} %convert_bitcast_fusion.2) | data formatting | bytes 2949120 | tf_op jit(solution)/shard_map/convert_element_type | solution.py:27
  86.2 7.2 %convert_element_type.66 = bf16[3,3,320,256]{3,2,1,0:T(8,128)(2,1)S(1)} reshape(bf16[3,3,10,32,8,32]{5,4,3,2,1,0:T(8,128)(2,1)} %copy.127) | data formatting | bytes 2949120 | tf_op jit(solution)/shard_map/convert_element_type | solution.py:27
  93.7 10.3 %copy.141 = bf16[3,3,10,32,8,32]{5,4,3,2,1,0:T(8,128)(2,1)} copy(bf16[3,3,10,32,8,32]{5,2,3,1,0,4:T(8,128)(2,1)} %convert_bitcast_fusion) | data formatting | bytes 2949120 | tf_op jit(solution)/shard_map/convert_element_type | solution.py:27
  103.9 8.3 %convert_element_type.74 = bf16[3,3,320,256]{3,2,1,0:T(8,128)(2,1)} reshape(bf16[3,3,10,32,8,32]{5,4,3,2,1,0:T(8,128)(2,1)} %copy.141) | data formatting | bytes 2949120 | tf_op jit(solution)/shard_map/convert_element_type | solution.py:27
  112.2 10.4 %copy.134 = bf16[3,3,10,32,8,32]{5,4,3,2,1,0:T(8,128)(2,1)} copy(bf16[3,3,10,32,8,32]{5,2,3,1,0,4:T(8,128)(2,1)} %convert_bitcast_fusion.1) | data formatting | bytes 2949120 | tf_op jit(solution)/shard_map/convert_element_type | solution.py:27
  122.6 7.2 %convert_element_type.70 = bf16[3,3,320,256]{3,2,1,0:T(8,128)(2,1)S(1)} reshape(bf16[3,3,10,32,8,32]{5,4,3,2,1,0:T(8,128)(2,1)} %copy.134) | data formatting | bytes 2949120 | tf_op jit(solution)/shard_map/convert_element_type | solution.py:27
  134.0 2.2 gather_fusion.2
  142.1 3.0 scatter.60
  145.1 2.9 scatter.61
  148.0 4.0 scatter.64
  152.0 4.0 scatter.65
  156.0 2.9 scatter.66
  158.9 5.7 scatter.69
  170.4 4.0 collective-permute-start.2
  182.9 2.7 scatter.84
  185.6 2.7 scatter.85
  189.0 5.0 scatter.89
  215.4 2.7 scatter.74
  218.1 2.7 scatter.75
  221.5 5.4 scatter.79
  231.5 2.2 fusion.72
  235.2 2.2 fusion.75
  239.0 2.2 fusion.78
  274.7 2.2 fusion.45
  282.3 264.0 %all-reduce.8.cloned.1.call-done = (f32[27,32,32]{2,1,0:T(8,128)}, f32[27,32,32]{2,1,0:T(8,128)}) async-done(((f32[27,32,32]{2,1,0:T(8,128)}, f32[27,32,32]{2,1,0:T(8,128)}), (f32[27,32,32]{2,1,0:T(8,128)}, f32[27,32,32]{2,1,0:T(8,128)})) %all-reduce.8.cloned.1.call-update) | async-done | bytes 221200 | tf_op jit(solution)/shard_map/psum | solution.py:163
  547.2 82.5 %all-reduce.10.cloned.1.call-done = (f32[27,32,32]{2,1,0:T(8,128)}, f32[27,32,32]{2,1,0:T(8,128)}) async-done(((f32[27,32,32]{2,1,0:T(8,128)}, f32[27,32,32]{2,1,0:T(8,128)}), (f32[27,32,32]{2,1,0:T(8,128)}, f32[27,32,32]{2,1,0:T(8,128)})) %all-reduce.10.cloned.1.call-update) | async-done | bytes 221200 | tf_op jit(solution)/shard_map/psum | solution.py:163
  (272 shorter events, 121.6 us)
Async XLA Ops:
  7.2 16.7 %copy-start = (bf16[1,64,512]{2,1,0:T(8,128)(2,1)S(1)}, bf16[1,64,512]{2,1,0:T(8,128)(2,1)}, u32[]{:S(2)}) copy-start(bf16[1,64,512]{2,1,0:T(8,128)(2,1)} %param.45) | copy-start | bytes 196612
  7.2 38.3 %copy-start.8 = (bf16[27,32,32]{2,1,0:T(8,128)(2,1)S(1)}, bf16[27,32,32]{2,1,0:T(8,128)(2,1)}, u32[]{:S(2)}) copy-start(bf16[27,32,32]{2,1,0:T(8,128)(2,1)} %param.50) | copy-start | bytes 165892
  13.7 162.2 %collective-permute-start.4 = (bf16[1,2,6,2048]{3,1,2,0:T(2,128)(2,1)}, bf16[1,2,6,2048]{3,1,2,0:T(2,128)(2,1)}, u32[]{:S(2)}, u32[]{:S(2)}) collective-permute-start(bf16[1,2,6,2048]{3,1,2,0:T(2,128)(2,1)} %bitcast.92), channel_id=1, source_target_pairs={{0,8},{8,16},{16,24},{24,32},{32,40},{40,48},{48,56},{56,64},{64,7... | collective-permute-start | bytes 147464 | tf_op jit(solution)/shard_map/ppermute | solution.py:11
  18.7 157.2 %collective-permute-start.5 = (bf16[1,2,6,2048]{3,1,2,0:T(2,128)(2,1)}, bf16[1,2,6,2048]{3,1,2,0:T(2,128)(2,1)}, u32[]{:S(2)}, u32[]{:S(2)}) collective-permute-start(bf16[1,2,6,2048]{3,1,2,0:T(2,128)(2,1)} %bitcast.92), channel_id=1, source_target_pairs={{8,0},{16,8},{24,16},{32,24},{40,32},{48,40},{56,48},{64,56},{72,6... | collective-permute-start | bytes 147464 | tf_op jit(solution)/shard_map/ppermute | solution.py:11
  21.3 116.5 %copy-start.16 = (pred[2,6]{1,0:T(4,128)(4,1)}, pred[2,6]{1,0:T(4,128)(4,1)S(1)}, u32[]{:S(2)}) copy-start(pred[2,6]{1,0:T(4,128)(4,1)S(1)} %get-tuple-element.287) | copy-start | bytes 40
  23.8 112.4 %copy-start.14 = (pred[12]{0:T(512)(128)(4,1)}, pred[12]{0:T(512)(128)(4,1)S(1)}, u32[]{:S(2)}) copy-start(pred[12]{0:T(512)(128)(4,1)S(1)} %get-tuple-element.244) | copy-start | bytes 40
  25.9 33.5 %all-to-all-start = ((bf16[64,2,512]{2,1,0:T(2,128)(2,1)}), bf16[64,2,512]{2,1,0:T(2,128)(2,1)S(1)}, u32[]{:S(2)}, u32[]{:S(2)}) async-start(bf16[64,2,512]{2,1,0:T(2,128)(2,1)} %broadcast_select_fusion.1), calls=%async_computation | async-start | bytes 262144 | tf_op jit(solution)/shard_map/all_to_all | solution.py:138
  45.4 500.9 %all-reduce.8.cloned.1.call-start = ((), (), s32[]{:S(2)}) async-start(), calls=%async_computation.1 | async-start | bytes 1769472 | tf_op jit(solution)/shard_map/psum | solution.py:163
  45.5 5.6 copy-start.18
  45.5 5.7 copy-start.9
  45.5 6.0 copy-start.6
  61.2 68.5 %copy-start.4 = (bf16[2,8,8,256]{3,2,1,0:T(8,128)(2,1)}, bf16[2,8,8,256]{3,2,1,0:T(8,128)(2,1)S(1)}, u32[]{:S(2)}) copy-start(bf16[2,8,8,256]{3,2,1,0:T(8,128)(2,1)S(1)} %convert_element_type.62) | copy-start | bytes 196612
  65.3 65.3 %collective-permute-start = (bf16[1,2,6,2048]{3,1,2,0:T(2,128)(2,1)}, bf16[1,2,6,2048]{3,1,2,0:T(2,128)(2,1)}, u32[]{:S(2)}, u32[]{:S(2)}) collective-permute-start(bf16[1,2,6,2048]{3,1,2,0:T(2,128)(2,1)} %bitcast.10), channel_id=1, source_target_pairs={{0,8},{8,16},{16,24},{24,32},{32,40},{40,48},{48,56},{56,64},{64,7... | collective-permute-start | bytes 147464 | tf_op jit(solution)/shard_map/ppermute | solution.py:11
  68.5 62.1 %collective-permute-start.1 = (bf16[1,2,6,2048]{3,1,2,0:T(2,128)(2,1)}, bf16[1,2,6,2048]{3,1,2,0:T(2,128)(2,1)}, u32[]{:S(2)}, u32[]{:S(2)}) collective-permute-start(bf16[1,2,6,2048]{3,1,2,0:T(2,128)(2,1)} %bitcast.10), channel_id=1, source_target_pairs={{8,0},{16,8},{24,16},{32,24},{40,32},{48,40},{56,48},{64,56},{72,6... | collective-permute-start | bytes 147464 | tf_op jit(solution)/shard_map/ppermute | solution.py:11
  86.2 7.2 %copy-start.7 = (bf16[1,2,8,8,256]{4,3,2,1,0:T(8,128)(2,1)S(1)}, bf16[1,2,8,8,256]{4,3,2,1,0:T(8,128)(2,1)}, u32[]{:S(2)}) copy-start(bf16[1,2,8,8,256]{4,3,2,1,0:T(8,128)(2,1)} %param.48) | copy-start | bytes 196612
  164.6 3.4 copy-start.2
  170.4 7.5 %collective-permute-start.2 = (bf16[1,2,6,2048]{3,1,2,0:T(2,128)(2,1)S(1)}, bf16[1,2,6,2048]{3,1,2,0:T(2,128)(2,1)S(1)}, u32[]{:S(2)}, u32[]{:S(2)}) collective-permute-start(bf16[1,2,6,2048]{3,1,2,0:T(2,128)(2,1)S(1)} %bitcast.663), channel_id=1, source_target_pairs={{0,8},{8,16},{16,24},{24,32},{32,40},{40,48},{48,56},{56,64},{64,7... | collective-permute-start | bytes 147464 | tf_op jit(solution)/shard_map/ppermute | solution.py:11
  174.3 4.8 collective-permute-start.3
  177.0 3.1 copy-start.15
  177.1 3.2 copy-start.17
  196.2 6.7 %copy-start.19 = (f32[2,8,8,256]{3,2,1,0:T(8,128)S(1)}, f32[2,8,8,256]{3,2,1,0:T(8,128)}, u32[]{:S(2)}) copy-start(f32[2,8,8,256]{3,2,1,0:T(8,128)} %get-tuple-element.296) | copy-start | bytes 393220
  199.6 4.5 copy-start.3
  250.8 1.6 copy-start.10
  250.9 1.6 copy-start.11
  250.9 1.6 copy-start.12
  278.2 1.6 copy-start.13
  281.8 264.5 %copy-start.5 = (bf16[2,8,8,256]{3,2,1,0:T(8,128)(2,1)S(1)}, bf16[2,8,8,256]{3,2,1,0:T(8,128)(2,1)}, u32[]{:S(2)}) copy-start(bf16[2,8,8,256]{3,2,1,0:T(8,128)(2,1)} %copy-done.4) | copy-start | bytes 196612
  282.1 347.7 %all-reduce.10.cloned.1.call-start = ((), (), s32[]{:S(2)}) async-start(), calls=%async_computation.2 | async-start | bytes 1769472 | tf_op jit(solution)/shard_map/psum | solution.py:163
  546.3 87.0 %copy-start.1 = (bf16[1,64,512]{2,1,0:T(8,128)(2,1)S(1)}, bf16[1,64,512]{2,1,0:T(8,128)(2,1)}, u32[]{:S(2)}) copy-start(bf16[1,64,512]{2,1,0:T(8,128)(2,1)} %param.45) | copy-start | bytes 196612
Sparse Core Ops, SparseCore 0:
  282.2 264.1 all-reduce.7
  549.0 80.6 all-reduce.9
